TPU v7x, 256 devices: a whole 4x4x8 slice. The times are simulated.
256 devices in a mesh: sec: 2 (over z_hi), seq: 16 (over y, z_lo), tp: 8 (over x, core).
Axes of the slice: x: 4, y: 4, z: 8 (z_hi: 2, z_lo: 4; z = z_hi * 4 + z_lo), core: 2. Of those that a mesh axis runs over, the one named last changes fastest.
Arguments:
- hidden_context: bfloat16 [8192, 8192], P(('sec', 'seq'), 'tp')
- hidden_rows: bfloat16 [512, 8192], P(('sec', 'seq'), 'tp')
- norm_gain: float32 [8192], replicated, may hold values from 0.25 to 2
- key_value_weight: bfloat16 [8192, 2, 1024], P(None, None, 'tp'), may hold values from -0.0625 to 0.0625
- value_bias: float32 [1024], P('tp'), may hold values from -4 to 4
- query_context: bfloat16 [8192, 8192], P(('sec', 'seq'), 'tp')
- query_rows: bfloat16 [512, 8192], P(('sec', 'seq'), 'tp')
- context_length: int32 [512], P(('sec', 'seq')), may hold values from 1 to 8192, as said below
- row_node: int32 [512], replicated, may hold values from 0 to 255, never falling along the last dimension, each value on 1 to 4 neighbouring positions
Outputs:
- prefill_attended: bfloat16 [8192, 8192], P(('sec', 'seq'), 'tp')
- decode_attended: bfloat16 [512, 8192], P(('sec', 'seq'), 'tp')
Inputs may be any that keep to these rules, and one draw needn't show every extreme that they name: `context_length`: some row sees the whole context of 8192 tokens. `row_node`: never falls; each node holds 1 to 4 consecutive rows, and some node exactly 4.
All inputs are finite; a program needn't handle non-finite values.
Results may differ from a plain program's by a relative error of at most 0.012.
The roundings to bfloat16 on the way count: a program that leaves them out, or rounds other values in their place, can miss the bound.
Values may be sent and summed in bfloat16 or wider, within the bound.
No kernel may reach another device: no remote copies, remote signals or barrier semaphores. Data moves between devices by JAX's collectives and lax.ppermute only.
A program may use at most 64 MiB of HBM per device.

v0:
```python
import math

import jax
import jax.numpy as jnp
from jax import lax
from jax.sharding import PartitionSpec as P

D = 8192
H = 64
KVH = 8
HD = 128
STEPS = 4


LOWEST = -1e30


def shifted(block, axis, distance):
    devices = range(lax.axis_size(axis))
    route = [(i - distance, i) for i in devices if i - distance in devices]
    return lax.ppermute(block, axis, route)


def empty_state(heads, group, count):
    return (
        jnp.full((heads, group, count), LOWEST, jnp.float32),
        jnp.zeros((heads, group, count), jnp.float32),
        jnp.zeros((heads, group, count, HD), jnp.float32),
    )


def attend_block(state, queries, keys, values, allowed):
    running, total, mixed = state
    length = keys.shape[0]
    heads = queries.shape[1]
    key_heads = keys.reshape(length, heads, HD)
    value_heads = values.reshape(length, heads, HD)
    scores = jnp.einsum(
        "rkgd,nkd->kgrn", queries, key_heads, preferred_element_type=jnp.float32
    ) / math.sqrt(HD)
    scores = jnp.where(allowed, scores, LOWEST)
    highest = jnp.maximum(running, jnp.max(scores, axis=-1))
    weights = jnp.where(allowed, jnp.exp(scores - highest[..., None]), 0.0)
    factor = jnp.exp(running - highest)
    total = total * factor + jnp.sum(weights, axis=-1)
    update = jnp.einsum(
        "kgrn,nkd->kgrd",
        weights.astype(jnp.bfloat16),
        value_heads,
        preferred_element_type=jnp.float32,
    )
    return (highest, total, mixed * factor[..., None] + update)


def attend_piece(state, queries, keys, values, allow_fn):
    length = keys.shape[0]
    width = math.gcd(length, 1024)

    def advance(number, current):
        offset = number * width
        key_part = lax.dynamic_slice_in_dim(keys, offset, width, 0)
        value_part = lax.dynamic_slice_in_dim(values, offset, width, 0)
        positions = offset + jnp.arange(width, dtype=jnp.int32)
        return attend_block(current, queries, key_part, value_part, allow_fn(positions))

    return lax.fori_loop(0, length // width, advance, state)


def finish(state):
    result = state[2] / state[1][..., None]
    result = jnp.transpose(result, (2, 0, 1, 3))
    return result.reshape(result.shape[0], -1).astype(jnp.bfloat16)


def per_device(
    hidden_context,
    hidden_rows,
    norm_gain,
    key_value_weight,
    value_bias,
    query_context,
    query_rows,
    context_length,
    row_node,
):
    tokens = hidden_context.shape[0]
    scored = hidden_rows.shape[0]
    columns = key_value_weight.shape[2]
    heads = columns // HD
    group = H // KVH
    pieces = (
        lax.all_gather(hidden_context, "tp", axis=1, tiled=True),
        lax.all_gather(hidden_rows, "tp", axis=1, tiled=True),
    )
    length = pieces[0].shape[1]
    weights = key_value_weight.reshape(length, 2 * columns)
    result = []
    for number in range(2):
        wide = pieces[number].astype(jnp.float32)
        result.append(jnp.sum(wide * wide, axis=1))
        scaled = (wide * norm_gain).astype(jnp.bfloat16)
        result.append(jnp.dot(scaled, weights, preferred_element_type=jnp.float32))
    squares_context, product_context, squares_rows, product_rows = tuple(result)

    def split_pair(squares, product):
        inverse = lax.rsqrt(squares / D + 1e-06)[:, None]
        keys = (product[:, :columns] * inverse).astype(jnp.bfloat16)
        values = (product[:, columns:] * inverse + value_bias).astype(jnp.bfloat16)
        return (keys, values)

    key_context, value_context = split_pair(squares_context, product_context)
    key_rows, value_rows = split_pair(squares_rows, product_rows)
    queries_context = query_context.reshape(tokens, heads, group, HD)
    queries_rows = query_rows.reshape(scored, heads, group, HD)
    place = lax.axis_index(("sec", "seq"))
    token_positions = place * tokens + jnp.arange(tokens, dtype=jnp.int32)
    row_positions = place * scored + jnp.arange(scored, dtype=jnp.int32)

    def causal(positions):
        return positions[None, :] <= token_positions[:, None]

    def within(positions):
        return positions[None, :] < context_length[:, None]

    rim_keys, rim_values = shifted(
        (key_rows[scored - (STEPS - 1) :], value_rows[scored - (STEPS - 1) :]), ("sec", "seq"), 1
    )
    appended_keys = jnp.concatenate([rim_keys, key_rows], axis=0)
    appended_values = jnp.concatenate([rim_values, value_rows], axis=0)
    appended_positions = (
        place * scored - (STEPS - 1) + jnp.arange(STEPS - 1 + scored, dtype=jnp.int32)
    )
    padded_nodes = jnp.concatenate([jnp.full((STEPS - 1,), -1, jnp.int32), row_node], axis=0)
    appended_nodes = lax.dynamic_slice_in_dim(padded_nodes, place * scored, STEPS - 1 + scored, 0)
    own_nodes = lax.dynamic_slice_in_dim(row_node, place * scored, scored, 0)
    appended_ok = (appended_positions[None, :] <= row_positions[:, None]) & (
        appended_nodes[None, :] == own_nodes[:, None]
    )
    state_rows = attend_block(
        empty_state(heads, group, scored), queries_rows, appended_keys, appended_values, appended_ok
    )
    pieces = (
        lax.all_gather(key_context, ("sec", "seq"), axis=0, tiled=True),
        lax.all_gather(value_context, ("sec", "seq"), axis=0, tiled=True),
    )
    state_context = attend_piece(
        empty_state(heads, group, tokens), queries_context, pieces[0], pieces[1], causal
    )
    pieces = (
        lax.all_gather(key_context, ("sec", "seq"), axis=0, tiled=True),
        lax.all_gather(value_context, ("sec", "seq"), axis=0, tiled=True),
    )
    state_rows = attend_piece(state_rows, queries_rows, pieces[0], pieces[1], within)
    return (finish(state_context), finish(state_rows))


def solution(mesh):
    return jax.shard_map(
        per_device,
        mesh=mesh,
        in_specs=(
            P(("sec", "seq"), "tp"),
            P(("sec", "seq"), "tp"),
            P(),
            P(None, None, "tp"),
            P("tp"),
            P(("sec", "seq"), "tp"),
            P(("sec", "seq"), "tp"),
            P(("sec", "seq")),
            P(),
        ),
        out_specs=(P(("sec", "seq"), "tp"), P(("sec", "seq"), "tp")),
        check_vma=False,
    )
```

profile of v0, /device:TPU:240, one launch (start us, length us, event | category | flops | bytes accessed | tf_op | source)
XLA Modules:
  0.0 492.7 jit_solution(5095776001138696008)
XLA Ops:
  7.2 0.7 all-gather.4.cloned.1.call-update
  8.0 36.8 %all-gather.4.cloned.1.call-done = bf16[256,8192]{1,0:T(8,128)(2,1)} async-done(((bf16[256,1024]{1,0:T(8,128)(2,1)}), bf16[256,8192]{1,0:T(8,128)(2,1)}) %all-gather.4.cloned.1.call-update) | async-done | bytes 4194320 | tf_op jit(solution)/shard_map/all_gather | solution.py:92
  44.8 3.1 fusion.47
  47.9 4.8 fusion.48
  52.7 0.8 fusion.65
  53.5 0.7 all-gather.8.cloned.1.call-update
  54.2 12.8 %all_gather.17 = bf16[16,8192]{1,0:T(8,128)(2,1)S(1)} all-gather(bf16[16,1024]{1,0:T(8,128)(2,1)S(1)} %copy-done.3), channel_id=1, replica_groups=mesh['sec'=2,'seq'=16,'tp'=8] {'tp'}, dimensions={1}, use_global_device_ids=true | all-gather | bytes 294912 | tf_op jit(solution)/shard_map/all_gather | solution.py:93
  67.3 2.9 fusion.50
  70.2 5.5 %collective-permute-start = (bf16[3,128]{1,0:T(4,128)(2,1)S(1)}, bf16[3,128]{1,0:T(4,128)(2,1)S(1)}, u32[]{:S(2)}, u32[]{:S(2)}) collective-permute-start(bf16[3,128]{1,0:T(4,128)(2,1)S(1)} %slice.27), channel_id=1, source_target_pairs={{0,8},{8,16},{16,24},{24,32},{32,40},{40,48},{48,56},{56,64},{64,7... | collective-permute-start | bytes 2312 | tf_op jit(solution)/shard_map/ppermute | solution.py:21
  75.8 2.6 collective-permute-start.1
  79.6 1.7 collective-permute-done.1
  81.5 112.4 %all-gather.6.cloned.1.call-done = bf16[8192,128]{1,0:T(8,128)(2,1)} async-done(((bf16[256,128]{1,0:T(8,128)(2,1)}), bf16[8192,128]{1,0:T(8,128)(2,1)}) %all-gather.6.cloned.1.call-update) | async-done | bytes 2097168 | tf_op jit(solution)/shard_map/all_gather | solution.py:143
  193.9 143.6 %all-gather.8.cloned.1.call-done = bf16[8192,128]{1,0:T(8,128)(2,1)} async-done(((bf16[256,128]{1,0:T(8,128)(2,1)}), bf16[8192,128]{1,0:T(8,128)(2,1)}) %all-gather.8.cloned.1.call-update) | async-done | bytes 2097168 | tf_op jit(solution)/shard_map/all_gather | solution.py:144
  337.5 122.9 %while.36 = (s32[]{:T(128)}, f32[1,8,256]{2,1,0:T(8,128)S(1)}, f32[1,8,256]{2,1,0:T(8,128)S(1)}, f32[1,8,256,128]{3,2,1,0:T(8,128)S(1)}, bf16[8192,128]{1,0:T(8,...) while((s32[]{:T(128)}, f32[1,8,256]{2,1,0:T(8,128)S(1)}, ...), condition=%wide.region_4.5_spmd.clone, body=%wide.region_1.4_spmd.clone.sunk | while | flops 1102066944 | bytes 63056096 | solution.py:66
  337.8 5.6 %fusion.111 = (f32[8,256]{1,0:T(8,128)S(1)}, f32[1024,256,8]{1,0,2:T(8,128)}) fusion(pred[256,1024]{0,1:T(8,128)(4,1)S(1)} %broadcast_compare_fusion.5, bf16[256,1,8,128]{3,0,2,1:T(8,128)(2,1)S(1)} %get-tuple-element.526, bf16[8192,128]{1,0:T(8,128)(2,1)} %get-tuple-element.525, s32[]{:T(128)S(6)} %select_n.129), kind=kOutput, calls=%fused_computation.29.clone.1 | convolution fusion | flops 543160320 | bytes 9445380 | tf_op jit(solution)/shard_map/while/body/eval_jaxpr/rkgd,nkd->kgrn/dot_general | solution.py:38
  343.4 4.6 fusion.113
  348.0 1.2 copy-done
  349.2 3.7 fusion.114
  353.1 5.6 %fusion.111 = (f32[8,256]{1,0:T(8,128)S(1)}, f32[1024,256,8]{1,0,2:T(8,128)}) fusion(pred[256,1024]{0,1:T(8,128)(4,1)S(1)} %broadcast_compare_fusion.5, bf16[256,1,8,128]{3,0,2,1:T(8,128)(2,1)S(1)} %get-tuple-element.526, bf16[8192,128]{1,0:T(8,128)(2,1)} %get-tuple-element.525, s32[]{:T(128)S(6)} %select_n.129), kind=kOutput, calls=%fused_computation.29.clone.1 | convolution fusion | flops 543160320 | bytes 9445380 | tf_op jit(solution)/shard_map/while/body/eval_jaxpr/rkgd,nkd->kgrn/dot_general | solution.py:38
  358.7 4.6 fusion.113
  363.4 1.2 copy-done
  364.6 3.7 fusion.114
  368.5 5.6 %fusion.111 = (f32[8,256]{1,0:T(8,128)S(1)}, f32[1024,256,8]{1,0,2:T(8,128)}) fusion(pred[256,1024]{0,1:T(8,128)(4,1)S(1)} %broadcast_compare_fusion.5, bf16[256,1,8,128]{3,0,2,1:T(8,128)(2,1)S(1)} %get-tuple-element.526, bf16[8192,128]{1,0:T(8,128)(2,1)} %get-tuple-element.525, s32[]{:T(128)S(6)} %select_n.129), kind=kOutput, calls=%fused_computation.29.clone.1 | convolution fusion | flops 543160320 | bytes 9445380 | tf_op jit(solution)/shard_map/while/body/eval_jaxpr/rkgd,nkd->kgrn/dot_general | solution.py:38
  374.1 4.6 fusion.113
  378.8 1.2 copy-done
  379.9 3.7 fusion.114
  383.9 5.6 %fusion.111 = (f32[8,256]{1,0:T(8,128)S(1)}, f32[1024,256,8]{1,0,2:T(8,128)}) fusion(pred[256,1024]{0,1:T(8,128)(4,1)S(1)} %broadcast_compare_fusion.5, bf16[256,1,8,128]{3,0,2,1:T(8,128)(2,1)S(1)} %get-tuple-element.526, bf16[8192,128]{1,0:T(8,128)(2,1)} %get-tuple-element.525, s32[]{:T(128)S(6)} %select_n.129), kind=kOutput, calls=%fused_computation.29.clone.1 | convolution fusion | flops 543160320 | bytes 9445380 | tf_op jit(solution)/shard_map/while/body/eval_jaxpr/rkgd,nkd->kgrn/dot_general | solution.py:38
  389.5 4.6 fusion.113
  394.1 1.2 copy-done
  395.3 3.7 fusion.114
  399.2 5.6 %fusion.111 = (f32[8,256]{1,0:T(8,128)S(1)}, f32[1024,256,8]{1,0,2:T(8,128)}) fusion(pred[256,1024]{0,1:T(8,128)(4,1)S(1)} %broadcast_compare_fusion.5, bf16[256,1,8,128]{3,0,2,1:T(8,128)(2,1)S(1)} %get-tuple-element.526, bf16[8192,128]{1,0:T(8,128)(2,1)} %get-tuple-element.525, s32[]{:T(128)S(6)} %select_n.129), kind=kOutput, calls=%fused_computation.29.clone.1 | convolution fusion | flops 543160320 | bytes 9445380 | tf_op jit(solution)/shard_map/while/body/eval_jaxpr/rkgd,nkd->kgrn/dot_general | solution.py:38
  404.8 4.6 fusion.113
  409.5 1.2 copy-done
  410.7 3.7 fusion.114
  414.6 5.6 %fusion.111 = (f32[8,256]{1,0:T(8,128)S(1)}, f32[1024,256,8]{1,0,2:T(8,128)}) fusion(pred[256,1024]{0,1:T(8,128)(4,1)S(1)} %broadcast_compare_fusion.5, bf16[256,1,8,128]{3,0,2,1:T(8,128)(2,1)S(1)} %get-tuple-element.526, bf16[8192,128]{1,0:T(8,128)(2,1)} %get-tuple-element.525, s32[]{:T(128)S(6)} %select_n.129), kind=kOutput, calls=%fused_computation.29.clone.1 | convolution fusion | flops 543160320 | bytes 9445380 | tf_op jit(solution)/shard_map/while/body/eval_jaxpr/rkgd,nkd->kgrn/dot_general | solution.py:38
  420.2 4.6 fusion.113
  424.9 1.2 copy-done
  426.0 3.7 fusion.114
  430.0 5.6 %fusion.111 = (f32[8,256]{1,0:T(8,128)S(1)}, f32[1024,256,8]{1,0,2:T(8,128)}) fusion(pred[256,1024]{0,1:T(8,128)(4,1)S(1)} %broadcast_compare_fusion.5, bf16[256,1,8,128]{3,0,2,1:T(8,128)(2,1)S(1)} %get-tuple-element.526, bf16[8192,128]{1,0:T(8,128)(2,1)} %get-tuple-element.525, s32[]{:T(128)S(6)} %select_n.129), kind=kOutput, calls=%fused_computation.29.clone.1 | convolution fusion | flops 543160320 | bytes 9445380 | tf_op jit(solution)/shard_map/while/body/eval_jaxpr/rkgd,nkd->kgrn/dot_general | solution.py:38
  435.6 4.6 fusion.113
  440.2 1.2 copy-done
  441.4 3.7 fusion.114
  445.3 5.6 %fusion.111 = (f32[8,256]{1,0:T(8,128)S(1)}, f32[1024,256,8]{1,0,2:T(8,128)}) fusion(pred[256,1024]{0,1:T(8,128)(4,1)S(1)} %broadcast_compare_fusion.5, bf16[256,1,8,128]{3,0,2,1:T(8,128)(2,1)S(1)} %get-tuple-element.526, bf16[8192,128]{1,0:T(8,128)(2,1)} %get-tuple-element.525, s32[]{:T(128)S(6)} %select_n.129), kind=kOutput, calls=%fused_computation.29.clone.1 | convolution fusion | flops 543160320 | bytes 9445380 | tf_op jit(solution)/shard_map/while/body/eval_jaxpr/rkgd,nkd->kgrn/dot_general | solution.py:38
  451.0 4.6 fusion.113
  455.6 1.2 copy-done
  456.8 3.7 fusion.114
  461.1 0.9 copy.44
  462.0 23.4 %while.35 = (s32[]{:T(128)}, f32[1,8,16]{2,1,0:T(8,128)S(1)}, f32[1,8,16]{2,1,0:T(8,128)S(1)}, f32[1,8,16,128]{3,2,1,0:T(8,128)S(1)}, s32[16]{0:T(128)S(1)}, /*i...) while((s32[]{:T(128)}, f32[1,8,16]{2,1,0:T(8,128)S(1)}, ...), condition=%wide.region_11.12_spmd, body=%wide.region_8.11_spmd.sunk | while | flops 68339072 | bytes 2343159 | solution.py:66
  462.1 1.3 fusion.105
  463.7 1.3 fusion.108
  465.1 1.3 fusion.105
  466.6 1.3 fusion.108
  468.0 1.3 fusion.105
  469.5 1.3 fusion.108
  470.9 1.3 fusion.105
  472.4 1.3 fusion.108
  473.8 1.3 fusion.105
  475.4 1.3 fusion.108
  476.7 1.3 fusion.105
  478.3 1.3 fusion.108
  479.7 1.3 fusion.105
  481.2 1.3 fusion.108
  482.6 1.3 fusion.105
  484.1 1.3 fusion.108
  (150 shorter events, 7.8 us)
Async XLA Ops:
  7.2 37.6 %all-gather.4.cloned.1.call-start = ((), (), s32[]{:S(2)}) async-start(), calls=%async_computation | async-start | bytes 4718592 | tf_op jit(solution)/shard_map/all_gather | solution.py:92
  7.9 44.8 %copy-start.5 = (f32[128]{0:T(128)S(1)}, f32[128]{0:T(128)}, u32[]{:S(2)}) copy-start(f32[128]{0:T(128)} %param.17) | copy-start | bytes 1540
  7.9 46.3 %copy-start.3 = (bf16[16,1024]{1,0:T(8,128)(2,1)S(1)}, bf16[16,1024]{1,0:T(8,128)(2,1)}, u32[]{:S(2)}) copy-start(bf16[16,1024]{1,0:T(8,128)(2,1)} %param.14) | copy-start | bytes 98308
  7.9 59.4 %copy-start.7 = (f32[8192]{0:T(1024)S(1)}, f32[8192]{0:T(1024)}, u32[]{:S(2)}) copy-start(f32[8192]{0:T(1024)} %param.15) | copy-start | bytes 98308
  7.9 186.0 %all-gather.6.cloned.1.call-start = ((), (), s32[]{:S(2)}) async-start(), calls=%async_computation.1 | async-start | bytes 2162688 | tf_op jit(solution)/shard_map/all_gather | solution.py:143
  47.9 30.5 %copy-start.6 = (s32[512]{0:T(512)S(1)}, s32[512]{0:T(512)}, u32[]{:S(2)}) copy-start(s32[512]{0:T(512)} %param.21) | copy-start | bytes 6148
  47.9 30.7 %copy-start.1 = (bf16[256,1024]{1,0:T(8,128)(2,1)S(1)}, bf16[256,1024]{1,0:T(8,128)(2,1)}, u32[]{:S(2)}) copy-start(bf16[256,1024]{1,0:T(8,128)(2,1)} %param.18) | copy-start | bytes 1572868
  47.9 31.2 %copy-start.2 = (bf16[16,1024]{1,0:T(8,128)(2,1)S(1)}, bf16[16,1024]{1,0:T(8,128)(2,1)}, u32[]{:S(2)}) copy-start(bf16[16,1024]{1,0:T(8,128)(2,1)} %param.19) | copy-start | bytes 98308
  53.5 284.1 %all-gather.8.cloned.1.call-start = ((), (), s32[]{:S(2)}) async-start(), calls=%async_computation.2 | async-start | bytes 2162688 | tf_op jit(solution)/shard_map/all_gather | solution.py:144
  70.2 8.9 %collective-permute-start = (bf16[3,128]{1,0:T(4,128)(2,1)S(1)}, bf16[3,128]{1,0:T(4,128)(2,1)S(1)}, u32[]{:S(2)}, u32[]{:S(2)}) collective-permute-start(bf16[3,128]{1,0:T(4,128)(2,1)S(1)} %slice.27), channel_id=1, source_target_pairs={{0,8},{8,16},{16,24},{24,32},{32,40},{40,48},{48,56},{56,64},{64,7... | collective-permute-start | bytes 2312 | tf_op jit(solution)/shard_map/ppermute | solution.py:21
  75.8 5.5 %collective-permute-start.1 = (bf16[3,128]{1,0:T(4,128)(2,1)S(1)}, bf16[3,128]{1,0:T(4,128)(2,1)S(1)}, u32[]{:S(2)}, u32[]{:S(2)}) collective-permute-start(bf16[3,128]{1,0:T(4,128)(2,1)S(1)} %slice.29), channel_id=1, source_target_pairs={{0,8},{8,16},{16,24},{24,32},{32,40},{40,48},{48,56},{56,64},{64,7... | collective-permute-start | bytes 2312 | tf_op jit(solution)/shard_map/ppermute | solution.py:21
  337.5 124.5 %copy-start.4 = (s32[16]{0:T(128)S(1)}, s32[16]{0:T(128)}, u32[]{:S(2)}) copy-start(s32[16]{0:T(128)} %param.20) | copy-start | bytes 196
  343.4 5.8 %copy-start = (f32[1024,256,8]{1,0,2:T(8,128)S(1)}, f32[1024,256,8]{1,0,2:T(8,128)}, u32[]{:S(2)}) copy-start(f32[1024,256,8]{1,0,2:T(8,128)} %get-tuple-element.495) | copy-start | bytes 25165828 | tf_op jit(solution)/shard_map/while
  358.7 5.8 %copy-start = (f32[1024,256,8]{1,0,2:T(8,128)S(1)}, f32[1024,256,8]{1,0,2:T(8,128)}, u32[]{:S(2)}) copy-start(f32[1024,256,8]{1,0,2:T(8,128)} %get-tuple-element.495) | copy-start | bytes 25165828 | tf_op jit(solution)/shard_map/while
  374.1 5.8 %copy-start = (f32[1024,256,8]{1,0,2:T(8,128)S(1)}, f32[1024,256,8]{1,0,2:T(8,128)}, u32[]{:S(2)}) copy-start(f32[1024,256,8]{1,0,2:T(8,128)} %get-tuple-element.495) | copy-start | bytes 25165828 | tf_op jit(solution)/shard_map/while
  389.5 5.8 %copy-start = (f32[1024,256,8]{1,0,2:T(8,128)S(1)}, f32[1024,256,8]{1,0,2:T(8,128)}, u32[]{:S(2)}) copy-start(f32[1024,256,8]{1,0,2:T(8,128)} %get-tuple-element.495) | copy-start | bytes 25165828 | tf_op jit(solution)/shard_map/while
  404.8 5.8 %copy-start = (f32[1024,256,8]{1,0,2:T(8,128)S(1)}, f32[1024,256,8]{1,0,2:T(8,128)}, u32[]{:S(2)}) copy-start(f32[1024,256,8]{1,0,2:T(8,128)} %get-tuple-element.495) | copy-start | bytes 25165828 | tf_op jit(solution)/shard_map/while
  420.2 5.8 %copy-start = (f32[1024,256,8]{1,0,2:T(8,128)S(1)}, f32[1024,256,8]{1,0,2:T(8,128)}, u32[]{:S(2)}) copy-start(f32[1024,256,8]{1,0,2:T(8,128)} %get-tuple-element.495) | copy-start | bytes 25165828 | tf_op jit(solution)/shard_map/while
  435.6 5.8 %copy-start = (f32[1024,256,8]{1,0,2:T(8,128)S(1)}, f32[1024,256,8]{1,0,2:T(8,128)}, u32[]{:S(2)}) copy-start(f32[1024,256,8]{1,0,2:T(8,128)} %get-tuple-element.495) | copy-start | bytes 25165828 | tf_op jit(solution)/shard_map/while
  450.9 5.8 %copy-start = (f32[1024,256,8]{1,0,2:T(8,128)S(1)}, f32[1024,256,8]{1,0,2:T(8,128)}, u32[]{:S(2)}) copy-start(f32[1024,256,8]{1,0,2:T(8,128)} %get-tuple-element.495) | copy-start | bytes 25165828 | tf_op jit(solution)/shard_map/while
Sparse Core Ops, SparseCore 0:
  9.8 34.8 all-gather.3
  53.6 140.2 all-gather.5
  196.3 141.2 all-gather.7
where the time goes:
time: 501 us; the launch traced here: 493 us
  waiting for transfers between devices  296 us (59%)
  matrix products  102 us (20%)
  other arithmetic  46.4 us (9%)
  between operations  14 us (3%)
  blocking collectives  12.8 us (3%)
  local copies, waits for them, and re-layouts  12 us (2%)
  starting transfers between devices  8.22 us (2%)
    all_gather x1, waiting for transfers between devices, per_device(): lax.all_gather(value_context, ('sec', 'seq'), axis=0, tiled=True)  144 us
    all_gather x1, waiting for transfers between devices, per_device(): lax.all_gather(key_context, ('sec', 'seq'), axis=0, tiled=True)  112 us
    dot_general x17, matrix products, attend_block(): jnp.einsum('rkgd,nkd->kgrn', queries, key_heads, preferred_element_type=j...  55.1 us
    dot_general x17, matrix products, attend_block(): jnp.einsum('kgrn,nkd->kgrd', weights.astype(jnp.bfloat16), value_heads, p...  39.5 us
    reduce_sum x17, other arithmetic, attend_block(): total = total * factor + jnp.sum(weights, axis=-1)  38.9 us
    all_gather x1, waiting for transfers between devices, per_device(): lax.all_gather(hidden_context, 'tp', axis=1, tiled=True)  36.8 us
    all_gather x1, blocking collectives, per_device(): lax.all_gather(hidden_rows, 'tp', axis=1, tiled=True)  12.8 us
  transfers between devices with their start and end apart: 5, of which 4 were waited for; matrix products, arithmetic and copies ran while one was open for 1% of the time, Pallas kernels for 0%

commit v1 on v0

v1 whole, which is shorter than its diff:
```python
import functools
import math

import jax
import jax.numpy as jnp
from jax import lax
from jax.experimental import pallas as pl
from jax.experimental.pallas import tpu as pltpu
from jax.sharding import PartitionSpec as P

D = 8192
H = 64
KVH = 8
HD = 128
STEPS = 4
GROUP = H // KVH

PLACE = ("sec", "seq")
RING_Z, RING_Y, RUN = 8, 4, 4
TOK = 256
ROW = 16
BOTH = TOK + ROW
TOP = 128
LOWEST = -1e30
SCALE = math.log2(math.e) / math.sqrt(HD)
VMEM = 48 * 1024 * 1024


def place_of(y, z):
    return (z // RUN) * (RING_Y * RUN) + y * RUN + z % RUN


def move(block, dz, dy):
    route = [
        (place_of(y, z), place_of((y + dy) % RING_Y, (z + dz) % RING_Z))
        for y in range(RING_Y)
        for z in range(RING_Z)
    ]
    return lax.ppermute(block, PLACE, route)


def move_x(block, step):
    return lax.ppermute(block, "tp", [(i, (i + 2 * step) % 8) for i in range(8)])


def swap_core(block):
    return lax.ppermute(block, "tp", [(i, i ^ 1) for i in range(8)])


def project_kernel(count, first, last, owners, *refs):
    refs = list(refs)
    pieces = [refs.pop(0) for _ in range(count)]
    weights = [refs.pop(0) for _ in range(count)]
    gain = refs.pop(0)
    if not first:
        product_in, squares_in = refs.pop(0), refs.pop(0)
    if last:
        bias = refs.pop(0)
    product = jnp.zeros((BOTH, 2 * HD), jnp.float32) if first else product_in[...]
    squares = jnp.zeros((BOTH, HD), jnp.float32) if first else squares_in[...]
    for number in range(count):
        own_gain = gain[pl.ds(owners[number], 1), :]
        for begin in range(0, 1024, 256):
            wide = pieces[number][:, begin : begin + 256].astype(jnp.float32)
            squared = wide * wide
            squares = squares + (squared[:, :HD] + squared[:, HD:])
            scaled = (wide * own_gain[:, begin : begin + 256]).astype(jnp.bfloat16)
            product = product + jnp.dot(
                scaled,
                weights[number][begin : begin + 256, :],
                preferred_element_type=jnp.float32,
            )
    if not last:
        refs[0][...] = product
        refs[1][...] = squares
        return
    inverse = lax.rsqrt(jnp.sum(squares, axis=1, keepdims=True) / D + 1e-06)
    keys = (product[:, :HD] * inverse).astype(jnp.bfloat16)
    values = (product[:, HD:] * inverse + bias[...]).astype(jnp.bfloat16)
    refs[0][:, :HD] = keys[:TOK]
    refs[0][:, HD:] = values[:TOK]
    refs[1][:, :HD] = keys[TOK:]
    refs[1][:, HD:] = values[TOK:]


def project(pieces, owners, weights, gain, state, bias):
    count = len(pieces)
    first, last = state is None, bias is not None

    def whole(array):
        return pl.BlockSpec(array.shape, lambda i, own: (0,) * array.ndim)

    operands = list(pieces) + [weights] * count + [gain]
    specs = [whole(piece) for piece in pieces]
    for number in range(count):
        specs.append(
            pl.BlockSpec((1024, 2 * HD), functools.partial(lambda j, i, own: (own[j], 0), number))
        )
    specs.append(whole(gain))
    if not first:
        operands += list(state)
        specs += [whole(array) for array in state]
    if last:
        operands.append(bias)
        specs.append(whole(bias))
        shapes = [
            jax.ShapeDtypeStruct((TOK, 2 * HD), jnp.bfloat16),
            jax.ShapeDtypeStruct((ROW, 2 * HD), jnp.bfloat16),
        ]
    else:
        shapes = [
            jax.ShapeDtypeStruct((BOTH, 2 * HD), jnp.float32),
            jax.ShapeDtypeStruct((BOTH, HD), jnp.float32),
        ]
    return pl.pallas_call(
        functools.partial(project_kernel, count, first, last),
        grid_spec=pltpu.PrefetchScalarGridSpec(
            num_scalar_prefetch=1,
            grid=(1,),
            in_specs=specs,
            out_specs=[whole(shape) for shape in shapes],
        ),
        out_shape=shapes,
        compiler_params=pltpu.CompilerParams(vmem_limit_bytes=VMEM),
        cost_estimate=pl.CostEstimate(
            flops=count * BOTH * 1024 * 512, bytes_accessed=count * 1100000, transcendentals=0
        ),
    )(owners, *operands)


def attend(queries, keys, values, allowed, top_ref, mixed_ref):
    parts = []
    highest = None
    for number in range(len(keys)):
        scores = lax.dot_general(
            queries, keys[number], (((1,), (1,)), ((), ())), preferred_element_type=jnp.float32
        )
        scores = scores * SCALE
        if allowed is not None:
            scores = jnp.where(allowed[number], scores, LOWEST)
        parts.append(scores)
        for begin in range(0, scores.shape[1], HD):
            piece = scores[:, begin : begin + HD]
            highest = piece if highest is None else jnp.maximum(highest, piece)
    before = top_ref[...]
    top = jnp.maximum(before, jnp.max(highest, axis=1, keepdims=True))
    factor = jnp.exp2(before - top)
    mixed = mixed_ref[...] * jnp.concatenate([factor, factor], axis=1)
    for number in range(len(keys)):
        width = parts[number].shape[1]
        lifted = jnp.concatenate([top] * (width // HD), axis=1)
        weight = jnp.exp2(parts[number] - lifted)
        if allowed is not None:
            weight = jnp.where(allowed[number], weight, 0.0)
        mixed = mixed + jnp.dot(
            weight.astype(jnp.bfloat16), values[number], preferred_element_type=jnp.float32
        )
    top_ref[...] = top
    mixed_ref[...] = mixed


def stage_kernel(lines, sizes, first, last, info, *refs):
    refs = list(refs)
    blocks = [refs.pop(0) for _ in sizes]
    query, query_rows, lengths = refs.pop(0), refs.pop(0), refs.pop(0)
    if first:
        extra, extra_ok = refs.pop(0), refs.pop(0)
    else:
        top_in, mixed_in, top_rows_in, mixed_rows_in = (refs.pop(0) for _ in range(4))
    if last:
        out, out_rows = refs.pop(0), refs.pop(0)
        keys, values, top_ref, mixed_ref, top_rows, mixed_rows = refs
    else:
        top_ref, mixed_ref, top_rows, mixed_rows, keys, values = refs
    step = pl.program_id(0)
    place, longest = info[0], info[1]

    @pl.when(step == 0)
    def _():
        number = 0
        for block, size in zip(blocks, sizes):
            for begin in range(0, size, TOK):
                spot = pl.multiple_of(info[8 + number] * TOK, TOK)
                keys[pl.ds(spot, TOK), :] = block[begin : begin + TOK, :HD]
                values[pl.ds(spot, TOK), :HD] = block[begin : begin + TOK, HD:]
                number += 1
        values[:, HD:] = jnp.ones((values.shape[0], HD), jnp.bfloat16)

    def parts_of(group):
        spans = [slice((4 * group + i) * TOK, (4 * group + i + 1) * TOK) for i in range(4)]
        return [keys[span, :] for span in spans], [values[span, :] for span in spans]

    @pl.when(step < GROUP)
    def _():
        if first:
            top_ref[...] = jnp.full(top_ref.shape, LOWEST, jnp.float32)
            mixed_ref[...] = jnp.zeros(mixed_ref.shape, jnp.float32)
        else:
            top_ref[...] = top_in[...]
            mixed_ref[...] = mixed_in[...]
        for group in range(2 * lines):
            number = info[2 + group]

            @pl.when(number < place // RUN)
            def _(group=group):
                some_keys, some_values = parts_of(group)
                attend(query[...], some_keys, some_values, None, top_ref, mixed_ref)

            if first:

                @pl.when(number == place // RUN)
                def _(group=group):
                    some_keys, some_values = parts_of(group)
                    tokens = lax.broadcasted_iota(jnp.int32, (TOK, TOK), 0) + (place % RUN) * TOK
                    offsets = lax.broadcasted_iota(jnp.int32, (TOK, TOK), 1)
                    allowed = [offsets + i * TOK <= tokens for i in range(4)]
                    attend(query[...], some_keys, some_values, allowed, top_ref, mixed_ref)

        if last:
            mixed = mixed_ref[...]
            out[...] = (mixed[:, :HD] / mixed[:, HD:]).astype(out.dtype)

    @pl.when(step == GROUP)
    def _():
        if first:
            top_rows[...] = jnp.full(top_rows.shape, LOWEST, jnp.float32)
            mixed_rows[...] = jnp.zeros(mixed_rows.shape, jnp.float32)
            extra_values = jnp.concatenate(
                [extra[:, HD:], jnp.ones((extra.shape[0], HD), jnp.bfloat16)], axis=1
            )
            attend(
                query_rows[...],
                [extra[:, :HD]],
                [extra_values],
                [extra_ok[...] > 0],
                top_rows,
                mixed_rows,
            )
        else:
            top_rows[...] = top_rows_in[...]
            mixed_rows[...] = mixed_rows_in[...]
        for group in range(2 * lines):
            number = info[2 + group]

            @pl.when(number * (RUN * TOK) < longest)
            def _(group=group, number=number):
                some_keys, some_values = parts_of(group)
                reach = lengths[...] - number * (RUN * TOK)
                reach = jnp.concatenate([reach, reach], axis=1)
                offsets = lax.broadcasted_iota(jnp.int32, reach.shape, 1)
                allowed = [offsets + i * TOK < reach for i in range(4)]
                attend(query_rows[...], some_keys, some_values, allowed, top_rows, mixed_rows)

        if last:
            mixed = mixed_rows[...]
            out_rows[...] = (mixed[:, :HD] / mixed[:, HD:]).astype(out_rows.dtype)


def stage(lines, info, blocks, query, query_rows, lengths, extra, state, last):
    first = state is None
    sizes = [block.shape[0] for block in blocks]

    def whole(array):
        return pl.BlockSpec(array.shape, lambda i, info: (0,) * len(array.shape))

    def down(width):
        return pl.BlockSpec((TOK, width), lambda i, info: (jnp.minimum(i, GROUP - 1), 0))

    across = pl.BlockSpec((TOK, HD), lambda i, info: (0, jnp.minimum(i, GROUP - 1)))
    operands = list(blocks) + [query, query_rows, lengths]
    specs = [whole(block) for block in blocks] + [across, whole(query_rows), whole(lengths)]
    state_shapes = [
        jax.ShapeDtypeStruct((GROUP * TOK, HD), jnp.float32),
        jax.ShapeDtypeStruct((GROUP * TOK, 2 * HD), jnp.float32),
        jax.ShapeDtypeStruct((GROUP * ROW, HD), jnp.float32),
        jax.ShapeDtypeStruct((GROUP * ROW, 2 * HD), jnp.float32),
    ]
    state_specs = [down(HD), down(2 * HD), whole(state_shapes[2]), whole(state_shapes[3])]
    if first:
        operands += list(extra)
        specs += [whole(array) for array in extra]
    else:
        operands += list(state)
        specs += state_specs
    scratch = [
        pltpu.VMEM((lines * RING_Z * TOK, HD), jnp.bfloat16),
        pltpu.VMEM((lines * RING_Z * TOK, 2 * HD), jnp.bfloat16),
    ]
    if last:
        shapes = [
            jax.ShapeDtypeStruct((TOK, GROUP * HD), jnp.bfloat16),
            jax.ShapeDtypeStruct((GROUP * ROW, HD), jnp.bfloat16),
        ]
        out_specs = [across, whole(shapes[1])]
        scratch += [
            pltpu.VMEM((TOK, HD), jnp.float32),
            pltpu.VMEM((TOK, 2 * HD), jnp.float32),
            pltpu.VMEM((GROUP * ROW, HD), jnp.float32),
            pltpu.VMEM((GROUP * ROW, 2 * HD), jnp.float32),
        ]
    else:
        shapes, out_specs = state_shapes, state_specs
    work = lines * RING_Z * TOK * TOK * GROUP
    return pl.pallas_call(
        functools.partial(stage_kernel, lines, sizes, first, last),
        grid_spec=pltpu.PrefetchScalarGridSpec(
            num_scalar_prefetch=1,
            grid=(GROUP + 1,),
            in_specs=specs,
            out_specs=out_specs,
            scratch_shapes=scratch,
        ),
        out_shape=shapes,
        compiler_params=pltpu.CompilerParams(vmem_limit_bytes=VMEM),
        cost_estimate=pl.CostEstimate(
            flops=work * 4 * HD * 2, bytes_accessed=4000000, transcendentals=work
        ),
    )(info, *operands)


def per_device(
    hidden_context,
    hidden_rows,
    norm_gain,
    key_value_weight,
    value_bias,
    query_context,
    query_rows,
    context_length,
    row_node,
):
    weights = key_value_weight.reshape(D, 2 * HD)
    gain = norm_gain.reshape(8, 1024)
    bias = value_bias.reshape(1, HD)
    tp = lax.axis_index("tp")
    place = lax.axis_index(PLACE)

    own = jnp.concatenate([hidden_context, hidden_rows], axis=0)
    low = move_x(own, 1)
    high = move_x(own, -1)
    twin = swap_core(own)
    across = [move_x(low[:TOP], 1), move_x(high[TOP:], -1)]
    low_twin = swap_core(low)
    high_twin = swap_core(high)
    far = jnp.concatenate(across, axis=0)
    far_twin = swap_core(far)
    mate = tp ^ 1

    def owners(*places):
        return jnp.stack([place % 8 for place in places]).astype(jnp.int32)

    state = project([own, twin], owners(tp, mate), weights, gain, None, None)
    state = project(
        [low, high, low_twin, high_twin],
        owners(tp + 6, tp + 2, mate + 6, mate + 2),
        weights,
        gain,
        state,
        None,
    )
    pairs, row_pairs = project(
        [far, far_twin], owners(tp + 4, mate + 4), weights, gain, state, bias
    )

    above, below = pairs, pairs
    pieces = [pairs]
    for _ in range(3):
        above, below = move(above, 1, 0), move(below, -1, 0)
        pieces += [above, below]
    pieces += [move(above[: TOK // 2], 1, 0), move(below[TOK // 2 :], -1, 0)]
    line = jnp.concatenate(pieces, axis=0)
    half = line.shape[0] // 2
    line_before = move(line, 0, 1)
    line_after = move(line, 0, -1)
    line_far = [move(line_before[:half], 0, 1), move(line_after[half:], 0, -1)]

    rim = lax.ppermute(row_pairs, PLACE, [(i, i + 1) for i in range(31)])
    nodes = row_node.reshape(-1, ROW)
    own_nodes = lax.dynamic_index_in_dim(nodes, place, 0, keepdims=False)
    rim_nodes = lax.dynamic_index_in_dim(nodes, jnp.maximum(place - 1, 0), 0, keepdims=False)
    rim_nodes = jnp.where(place > 0, rim_nodes, -1)
    seats = jnp.arange(ROW, dtype=jnp.int32)
    seat_ok = jnp.concatenate(
        [
            rim_nodes[None, :] == own_nodes[:, None],
            (seats[None, :] <= seats[:, None]) & (own_nodes[None, :] == own_nodes[:, None]),
            jnp.zeros((ROW, HD - 2 * ROW), bool),
        ],
        axis=1,
    )
    extra = (
        jnp.concatenate([rim, row_pairs, jnp.zeros((HD - 2 * ROW, 2 * HD), jnp.bfloat16)], axis=0),
        jnp.repeat(seat_ok.astype(jnp.float32), GROUP, axis=0),
    )
    reach = jnp.broadcast_to(context_length[:, None, None], (ROW, GROUP, HD))
    reach = reach.reshape(ROW * GROUP, HD)
    longest = jnp.max(context_length)
    row_queries = query_rows.reshape(ROW * GROUP, HD)

    y = (place // RUN) % RING_Y
    z = (place // (RING_Y * RUN)) * RUN + place % RUN
    order = jnp.array([0, 7, 1, 6, 2, 5, 3, 4], jnp.int32)
    spots = (z + order) % RING_Z

    def info(*ys):
        groups = [jnp.stack([yy % RING_Y, RING_Y + yy % RING_Y]) for yy in ys]
        groups = jnp.concatenate(groups + [jnp.zeros((6 - 2 * len(ys),), jnp.int32)])
        return jnp.concatenate(
            [jnp.stack([place, longest]), groups] + [spots + 8 * i for i in range(len(ys))]
        ).astype(jnp.int32)

    run = functools.partial(
        stage, query=query_context, query_rows=row_queries, lengths=reach
    )
    state = run(1, info(y), [line], extra=extra, state=None, last=False)
    state = run(2, info(y + 3, y + 1), [line_before, line_after], extra=None, state=state, last=False)
    out, out_rows = run(1, info(y + 2), line_far, extra=None, state=state, last=True)
    return out, out_rows.reshape(ROW, GROUP * HD)


def solution(mesh):
    return jax.shard_map(
        per_device,
        mesh=mesh,
        in_specs=(
            P(PLACE, "tp"),
            P(PLACE, "tp"),
            P(),
            P(None, None, "tp"),
            P("tp"),
            P(PLACE, "tp"),
            P(PLACE, "tp"),
            P(PLACE),
            P(),
        ),
        out_specs=(P(PLACE, "tp"), P(PLACE, "tp")),
        check_vma=False,
    )
```

time: 501 us -> 152 us (0.30)
  the two profiles are of different devices: /device:TPU:240 before, /device:TPU:158 now
where the time goes in v1:
time: 152 us; the launch traced here: 151 us
  Pallas kernels  70.6 us (46%)
  waiting for transfers between devices  34.5 us (23%)
  starting transfers between devices  24.4 us (16%)
  local copies, waits for them, and re-layouts  19 us (12%)
    pallas_call x3, Pallas kernels, stage(): pl.pallas_call(functools.partial(stage_kernel, lines, sizes, first, last)...  64.2 us
    ppermute x4, waiting for transfers between devices, move_x(): lax.ppermute(block, 'tp', [(i, (i + 2 * step) % 8) for i in range(8)])  19.5 us
    ppermute x12, starting transfers between devices, move(): return lax.ppermute(block, PLACE, route)  17.6 us
    unnamed x33, local copies, waits for them, and re-layouts  13 us
    ppermute x12, waiting for transfers between devices, move(): return lax.ppermute(block, PLACE, route)  11.8 us
    pallas_call x3, Pallas kernels, project(): pl.pallas_call(functools.partial(project_kernel, count, first, last), gri...  6.47 us
    ppermute x4, starting transfers between devices, move_x(): lax.ppermute(block, 'tp', [(i, (i + 2 * step) % 8) for i in range(8)])  4.13 us
    ppermute x1, waiting for transfers between devices, per_device(): rim = lax.ppermute(row_pairs, PLACE, [(i, i + 1) for i in range(31)])  3.18 us
  transfers between devices with their start and end apart: 21, of which 8 were waited for; matrix products, arithmetic and copies ran while one was open for 8% of the time, Pallas kernels for 35%

profile of v1, /device:TPU:158, one launch (start us, length us, event | category | flops | bytes accessed | tf_op | source)
XLA Modules:
  0.0 150.7 jit_solution(3401019225616725594)
XLA Ops:
  0.6 1.1 constant_dynamic-update-slice_fusion.1
  1.7 0.8 constant_dynamic-update-slice_fusion.refs_0_
  2.5 0.5 collective-permute-start
  3.0 1.5 %collective-permute-start.2 = (bf16[272,1024]{1,0:T(8,128)(2,1)S(1)}, bf16[272,1024]{1,0:T(8,128)(2,1)S(1)}, u32[]{:S(2)}, u32[]{:S(2)}) collective-permute-start(bf16[272,1024]{1,0:T(8,128)(2,1)S(1)} %constant_dynamic-update-slice_fusion.refs_0_), channel_id=1, source_target_pairs={{0,6},{1,7},{2,0},{3,1},{4,2},{5,3},{6,4},{7,5},{8,14},{9,15},{10,... | collective-permute-start | bytes 1671176 | tf_op jit(solution)/shard_map/ppermute | solution.py:43
  4.5 12.3 %collective-permute-done.refs_0_ = bf16[272,1024]{1,0:T(8,128)(2,1)S(1)} collective-permute-done((bf16[272,1024]{1,0:T(8,128)(2,1)S(1)}, bf16[272,1024]{1,0:T(8,128)(2,1)S(1)}, u32[]{:S(2)}, u32[]{:S(2)}) %collective-permute-start) | collective-permute-done | bytes 557088 | tf_op jit(solution)/shard_map/ppermute | solution.py:43
  16.9 1.8 %collective-permute-start.1 = (bf16[128,1024]{1,0:T(8,128)(2,1)S(1)}, bf16[128,1024]{1,0:T(8,128)(2,1)}, u32[]{:S(2)}, u32[]{:S(2)}) collective-permute-start(bf16[128,1024]{1,0:T(8,128)(2,1)S(1)} %slice.24), channel_id=1, source_target_pairs={{0,2},{1,3},{2,4},{3,5},{4,6},{5,7},{6,0},{7,1},{8,10},{9,11},{10,... | collective-permute-start | bytes 786440 | tf_op jit(solution)/shard_map/ppermute | solution.py:43
  18.6 0.7 slice.25
  19.4 0.3 collective-permute-start.3
  19.7 0.0 collective-permute-start.7
  19.7 0.1 pad_add_fusion.2.owners
  19.8 0.5 collective-permute-start.5
  20.3 0.1 collective-permute-start.6
  20.4 3.8 %collective-permute-done.1 = bf16[128,1024]{1,0:T(8,128)(2,1)} collective-permute-done((bf16[128,1024]{1,0:T(8,128)(2,1)S(1)}, bf16[128,1024]{1,0:T(8,128)(2,1)}, u32[]{:S(2)}, u32[]{:S(2)}) %collective-permute-start.1) | collective-permute-done | bytes 262176 | tf_op jit(solution)/shard_map/ppermute | solution.py:43
  24.2 1.0 constant_dynamic-update-slice_fusion.3
  25.2 3.3 %collective-permute-done.3 = bf16[144,1024]{1,0:T(8,128)(2,1)} collective-permute-done((bf16[144,1024]{1,0:T(8,128)(2,1)}, bf16[144,1024]{1,0:T(8,128)(2,1)}, u32[]{:S(2)}, u32[]{:S(2)}) %collective-permute-start.3) | collective-permute-done | bytes 294944 | tf_op jit(solution)/shard_map/ppermute | solution.py:43
  28.5 1.0 constant_dynamic-update-slice_fusion.2.refs_0_
  29.5 0.1 collective-permute-start.4
  29.6 0.1 pad_add_fusion.owners
  29.7 0.0 copy-start.8
  29.7 4.7 %copy.14 = bf16[1024,8,2,128]{3,1,2,0:T(8,128)(2,1)} copy(bf16[1024,8,2,128]{3,2,1,0:T(2,128)(2,1)} %bitcast.38) | data formatting | bytes 8388608
  34.4 0.1 reshape.34
  34.5 0.1 pad.2.clone
  34.6 0.1 pad_add_fusion.1.owners
  34.7 0.1 broadcast_compare_fusion
  34.8 2.2 %copy-done = bf16[1024,8,2,128]{3,1,2,0:T(8,128)(2,1)S(1)} copy-done((bf16[1024,8,2,128]{3,1,2,0:T(8,128)(2,1)S(1)}, bf16[1024,8,2,128]{3,1,2,0:T(8,128)(2,1)}, u32[]{:S(2)}) %copy-start) | copy-done | bytes 4194328
  36.9 1.0 shard_map.113
  38.0 0.0 copy-start.2
  38.0 3.3 %shard_map.114 = (f32[272,256]{1,0:T(8,128)S(1)}, f32[272,128]{1,0:T(8,128)S(1)}) custom-call(s32[4]{0:T(128)S(1)} %pad_add_fusion.1.owners, bf16[272,1024]{1,0:T(8,128)(2,1)S(1)} %collective-permute-done.refs_0_, bf16[272,1024]{1,0:T(8,128)(2,1)S(1)} %collective-permute-done.2.refs_1_, bf16[272,1024]{1,0:T(8,128)(2,1)S(1)} %collective-permute-done.5.refs_2_, ...), custom_call_target="tpu_custom_call" | custom-call | flops 570425344 | bytes 4400000 | tf_op jit(solution)/shard_map/pallas_call | solution.py:115
  41.4 0.0 copy-start.10
  41.4 0.0 copy-start.9
  41.4 0.0 copy-start.7
  41.4 2.1 %shard_map.115 = (bf16[256,256]{1,0:T(8,128)(2,1)S(1)}, bf16[16,256]{1,0:T(8,128)(2,1)S(1)}) custom-call(s32[2]{0:T(128)S(1)} %pad_add_fusion.owners, bf16[272,1024]{1,0:T(8,128)(2,1)S(1)} %constant_dynamic-update-slice_fusion.2.refs_0_, bf16[272,1024]{1,0:T(8,128)(2,1)} %collective-permute-done.4.refs_1_, bf16[8192,256]{1,0:T(8,128)(2,1)S(1)} %bitcast.35, ...), custom_call_target="tpu_custom_call" | custom-call | flops 285212672 | bytes 2200000 | tf_op jit(solution)/shard_map/pallas_call | solution.py:115
  43.5 1.1 collective-permute-start.8
  44.6 2.2 %collective-permute-start.9 = (bf16[256,256]{1,0:T(8,128)(2,1)S(1)}, bf16[256,256]{1,0:T(8,128)(2,1)S(1)}, u32[]{:S(2)}, u32[]{:S(2)}) collective-permute-start(bf16[256,256]{1,0:T(8,128)(2,1)S(1)} %get-tuple-element.22), channel_id=1, source_target_pairs={{0,152},{8,0},{16,8},{24,16},{128,24},{136,128},{144,136},{152,144... | collective-permute-start | bytes 393224 | tf_op jit(solution)/shard_map/ppermute | solution.py:39
  46.9 0.1 add_convert_fusion
  47.0 3.8 %collective-permute-done.8 = bf16[256,256]{1,0:T(8,128)(2,1)S(1)} collective-permute-done((bf16[256,256]{1,0:T(8,128)(2,1)S(1)}, bf16[256,256]{1,0:T(8,128)(2,1)S(1)}, u32[]{:S(2)}, u32[]{:S(2)}) %collective-permute-start.8) | collective-permute-done | bytes 131104 | tf_op jit(solution)/shard_map/ppermute | solution.py:39
  50.7 3.2 %collective-permute-start.11 = (bf16[256,256]{1,0:T(8,128)(2,1)S(1)}, bf16[256,256]{1,0:T(8,128)(2,1)S(1)}, u32[]{:S(2)}, u32[]{:S(2)}) collective-permute-start(bf16[256,256]{1,0:T(8,128)(2,1)S(1)} %collective-permute-done.9), channel_id=1, source_target_pairs={{0,152},{8,0},{16,8},{24,16},{128,24},{136,128},{144,136},{152,144... | collective-permute-start | bytes 393224 | tf_op jit(solution)/shard_map/ppermute | solution.py:39
  54.0 3.0 %collective-permute-done.10 = bf16[256,256]{1,0:T(8,128)(2,1)S(1)} collective-permute-done((bf16[256,256]{1,0:T(8,128)(2,1)S(1)}, bf16[256,256]{1,0:T(8,128)(2,1)S(1)}, u32[]{:S(2)}, u32[]{:S(2)}) %collective-permute-start.10) | collective-permute-done | bytes 131104 | tf_op jit(solution)/shard_map/ppermute | solution.py:39
  57.0 3.2 %collective-permute-start.13 = (bf16[256,256]{1,0:T(8,128)(2,1)S(1)}, bf16[256,256]{1,0:T(8,128)(2,1)S(1)}, u32[]{:S(2)}, u32[]{:S(2)}) collective-permute-start(bf16[256,256]{1,0:T(8,128)(2,1)S(1)} %collective-permute-done.11), channel_id=1, source_target_pairs={{0,152},{8,0},{16,8},{24,16},{128,24},{136,128},{144,136},{152,144... | collective-permute-start | bytes 393224 | tf_op jit(solution)/shard_map/ppermute | solution.py:39
  60.3 2.9 %collective-permute-done.12 = bf16[256,256]{1,0:T(8,128)(2,1)S(1)} collective-permute-done((bf16[256,256]{1,0:T(8,128)(2,1)S(1)}, bf16[256,256]{1,0:T(8,128)(2,1)S(1)}, u32[]{:S(2)}, u32[]{:S(2)}) %collective-permute-start.12) | collective-permute-done | bytes 131104 | tf_op jit(solution)/shard_map/ppermute | solution.py:39
  63.2 3.3 %collective-permute-start.15 = (bf16[128,256]{1,0:T(8,128)(2,1)S(1)}, bf16[128,256]{1,0:T(8,128)(2,1)S(1)}, u32[]{:S(2)}, u32[]{:S(2)}) collective-permute-start(bf16[128,256]{1,0:T(8,128)(2,1)S(1)} %slice.27), channel_id=1, source_target_pairs={{0,152},{8,0},{16,8},{24,16},{128,24},{136,128},{144,136},{152,144... | collective-permute-start | bytes 196616 | tf_op jit(solution)/shard_map/ppermute | solution.py:39
  66.6 2.1 %collective-permute-done.14 = bf16[128,256]{1,0:T(8,128)(2,1)S(1)} collective-permute-done((bf16[128,256]{1,0:T(8,128)(2,1)S(1)}, bf16[128,256]{1,0:T(8,128)(2,1)S(1)}, u32[]{:S(2)}, u32[]{:S(2)}) %collective-permute-start.14) | collective-permute-done | bytes 65568 | tf_op jit(solution)/shard_map/ppermute | solution.py:39
  68.7 0.3 collective-permute-start.16
  69.0 1.8 %collective-permute-start.18 = (bf16[2048,256]{1,0:T(8,128)(2,1)S(1)}, bf16[2048,256]{1,0:T(8,128)(2,1)S(1)}, u32[]{:S(2)}, u32[]{:S(2)}) collective-permute-start(bf16[2048,256]{1,0:T(8,128)(2,1)S(1)} %constant_dynamic-update-slice_fusion.4.refs_0_), channel_id=1, source_target_pairs={{0,96},{8,104},{16,112},{24,120},{128,224},{136,232},{144,240},{15... | collective-permute-start | bytes 3145736 | tf_op jit(solution)/shard_map/ppermute | solution.py:39
  70.8 1.9 %collective-permute-start.20 = (bf16[16,256]{1,0:T(8,128)(2,1)S(1)}, bf16[16,256]{1,0:T(8,128)(2,1)S(1)}, u32[]{:S(2)}, u32[]{:S(2)}) collective-permute-start(bf16[16,256]{1,0:T(8,128)(2,1)S(1)} %get-tuple-element.23), channel_id=1, source_target_pairs={{0,8},{8,16},{16,24},{24,32},{32,40},{40,48},{48,56},{56,64},{64,7... | collective-permute-start | bytes 24584 | tf_op jit(solution)/shard_map/ppermute | solution.py:377
  72.9 0.6 reduce_max.9
  73.5 0.1 broadcast_in_dim.29
  73.6 0.1 broadcast_in_dim.30
  73.7 0.1 pad.5.clone
  73.8 0.7 concatenate.29.info
  74.5 0.7 concatenate.24.info
  75.3 0.7 concatenate.28.info
  76.0 3.2 %collective-permute-done.20 = bf16[16,256]{1,0:T(8,128)(2,1)S(1)} collective-permute-done((bf16[16,256]{1,0:T(8,128)(2,1)S(1)}, bf16[16,256]{1,0:T(8,128)(2,1)S(1)}, u32[]{:S(2)}, u32[]{:S(2)}) %collective-permute-start.20) | collective-permute-done | bytes 8224 | tf_op jit(solution)/shard_map/ppermute | solution.py:377
  79.2 0.1 maximum_maximum_fusion.refs_4_
  79.3 0.1 broadcast_in_dim.31.refs_3_.refs_4_
  79.3 1.0 copy-done.3
  80.4 16.4 %shard_map.116 = (f32[2048,128]{1,0:T(8,128)S(1)}, f32[2048,256]{1,0:T(8,128)S(1)}, f32[128,128]{1,0:T(8,128)S(1)}, f32[128,256]{1,0:T(8,128)S(1)}) custom-call(s32[16]{0:T(128)S(1)} %concatenate.29.info, bf16[2048,256]{1,0:T(8,128)(2,1)S(1)} %constant_dynamic-update-slice_fusion.4.refs_0_, bf16[256,1024]{1,0:T(8,128)(2,1)S(1)} %copy-done.3, ...), custom_call_target="tpu_custom_call" | custom-call | flops 4294967296 | bytes 4000000 | tf_op jit(solution)/shard_map/pallas_call | solution.py:304
  96.8 1.4 copy-done.5
  98.2 2.1 %collective-permute-start.17 = (bf16[1024,256]{1,0:T(8,128)(2,1)S(1)}, bf16[1024,256]{1,0:T(8,128)(2,1)S(1)}, u32[]{:S(2)}, u32[]{:S(2)}) collective-permute-start(bf16[1024,256]{1,0:T(8,128)(2,1)S(1)} %slice.28), channel_id=1, source_target_pairs={{0,32},{8,40},{16,48},{24,56},{128,160},{136,168},{144,176},{152,1... | collective-permute-start | bytes 1572872 | tf_op jit(solution)/shard_map/ppermute | solution.py:39
  100.4 0.3 collective-permute-start.19
  100.7 31.4 %shard_map.117 = (f32[2048,128]{1,0:T(8,128)S(1)}, f32[2048,256]{1,0:T(8,128)}, f32[128,128]{1,0:T(8,128)S(1)}, f32[128,256]{1,0:T(8,128)S(1)}) custom-call(s32[24]{0:T(128)S(1)} %concatenate.28.info, bf16[2048,256]{1,0:T(8,128)(2,1)S(1)} %collective-permute-done.16.refs_0_, bf16[2048,256]{1,0:T(8,128)(2,1)S(1)} %collective-permute-done.18.refs_1_, ...), custom_call_target="tpu_custom_call" | custom-call | flops 8589934592 | bytes 4000000 | tf_op jit(solution)/shard_map/pallas_call | solution.py:304
  132.1 1.6 %copy-done.4 = f32[2048,256]{1,0:T(8,128)S(1)} copy-done((f32[2048,256]{1,0:T(8,128)S(1)}, f32[2048,256]{1,0:T(8,128)}, u32[]{:S(2)}) %copy-start.4) | copy-done | bytes 2097176
  133.7 16.3 %shard_map.118 = (bf16[256,1024]{1,0:T(8,128)(2,1)}, bf16[128,128]{1,0:T(8,128)(2,1)S(1)}) custom-call(s32[16]{0:T(128)S(1)} %concatenate.24.info, bf16[1024,256]{1,0:T(8,128)(2,1)S(1)} %collective-permute-done.17.refs_0_, bf16[1024,256]{1,0:T(8,128)(2,1)S(1)} %collective-permute-done.19.refs_1_, bf16[256,1024]{1,0:T(8,128)(2,1)S(1)} %copy-done.3, ...), custom_call_target="tpu_custom_call" | custom-call | flops 4294967296 | bytes 4000000 | tf_op jit(solution)/shard_map/pallas_call | solution.py:304
  150.0 0.6 reshape.36
  (52 shorter events, 0.3 us)
Async XLA Ops:
  2.5 14.4 %collective-permute-start = (bf16[272,1024]{1,0:T(8,128)(2,1)S(1)}, bf16[272,1024]{1,0:T(8,128)(2,1)S(1)}, u32[]{:S(2)}, u32[]{:S(2)}) collective-permute-start(bf16[272,1024]{1,0:T(8,128)(2,1)S(1)} %constant_dynamic-update-slice_fusion.refs_0_), channel_id=1, source_target_pairs={{0,2},{1,3},{2,4},{3,5},{4,6},{5,7},{6,0},{7,1},{8,10},{9,11},{10,... | collective-permute-start | bytes 1671176 | tf_op jit(solution)/shard_map/ppermute | solution.py:43
  3.0 15.7 %collective-permute-start.2 = (bf16[272,1024]{1,0:T(8,128)(2,1)S(1)}, bf16[272,1024]{1,0:T(8,128)(2,1)S(1)}, u32[]{:S(2)}, u32[]{:S(2)}) collective-permute-start(bf16[272,1024]{1,0:T(8,128)(2,1)S(1)} %constant_dynamic-update-slice_fusion.refs_0_), channel_id=1, source_target_pairs={{0,6},{1,7},{2,0},{3,1},{4,2},{5,3},{6,4},{7,5},{8,14},{9,15},{10,... | collective-permute-start | bytes 1671176 | tf_op jit(solution)/shard_map/ppermute | solution.py:43
  16.9 7.4 %collective-permute-start.1 = (bf16[128,1024]{1,0:T(8,128)(2,1)S(1)}, bf16[128,1024]{1,0:T(8,128)(2,1)}, u32[]{:S(2)}, u32[]{:S(2)}) collective-permute-start(bf16[128,1024]{1,0:T(8,128)(2,1)S(1)} %slice.24), channel_id=1, source_target_pairs={{0,2},{1,3},{2,4},{3,5},{4,6},{5,7},{6,0},{7,1},{8,10},{9,11},{10,... | collective-permute-start | bytes 786440 | tf_op jit(solution)/shard_map/ppermute | solution.py:43
  19.4 9.1 %collective-permute-start.3 = (bf16[144,1024]{1,0:T(8,128)(2,1)}, bf16[144,1024]{1,0:T(8,128)(2,1)}, u32[]{:S(2)}, u32[]{:S(2)}) collective-permute-start(bf16[144,1024]{1,0:T(8,128)(2,1)} %slice.25), channel_id=1, source_target_pairs={{0,6},{1,7},{2,0},{3,1},{4,2},{5,3},{6,4},{7,5},{8,14},{9,15},{10,... | collective-permute-start | bytes 884744 | tf_op jit(solution)/shard_map/ppermute | solution.py:43
  19.7 15.0 %collective-permute-start.7 = (bf16[272,1024]{1,0:T(8,128)(2,1)S(1)}, bf16[272,1024]{1,0:T(8,128)(2,1)S(1)}, u32[]{:S(2)}, u32[]{:S(2)}) collective-permute-start(bf16[272,1024]{1,0:T(8,128)(2,1)S(1)} %constant_dynamic-update-slice_fusion.refs_0_), channel_id=1, source_target_pairs={{0,1},{1,0},{2,3},{3,2},{4,5},{5,4},{6,7},{7,6},{8,9},{9,8},{10,11... | collective-permute-start | bytes 1671176 | tf_op jit(solution)/shard_map/ppermute | solution.py:47
  19.8 18.2 %collective-permute-start.5 = (bf16[272,1024]{1,0:T(8,128)(2,1)S(1)}, bf16[272,1024]{1,0:T(8,128)(2,1)S(1)}, u32[]{:S(2)}, u32[]{:S(2)}) collective-permute-start(bf16[272,1024]{1,0:T(8,128)(2,1)S(1)} %collective-permute-done.refs_0_), channel_id=1, source_target_pairs={{0,1},{1,0},{2,3},{3,2},{4,5},{5,4},{6,7},{7,6},{8,9},{9,8},{10,11... | collective-permute-start | bytes 1671176 | tf_op jit(solution)/shard_map/ppermute | solution.py:47
  20.3 17.7 %collective-permute-start.6 = (bf16[272,1024]{1,0:T(8,128)(2,1)S(1)}, bf16[272,1024]{1,0:T(8,128)(2,1)}, u32[]{:S(2)}, u32[]{:S(2)}) collective-permute-start(bf16[272,1024]{1,0:T(8,128)(2,1)S(1)} %collective-permute-done.2.refs_1_), channel_id=1, source_target_pairs={{0,1},{1,0},{2,3},{3,2},{4,5},{5,4},{6,7},{7,6},{8,9},{9,8},{10,11... | collective-permute-start | bytes 1671176 | tf_op jit(solution)/shard_map/ppermute | solution.py:47
  29.5 11.9 %collective-permute-start.4 = (bf16[272,1024]{1,0:T(8,128)(2,1)S(1)}, bf16[272,1024]{1,0:T(8,128)(2,1)}, u32[]{:S(2)}, u32[]{:S(2)}) collective-permute-start(bf16[272,1024]{1,0:T(8,128)(2,1)S(1)} %constant_dynamic-update-slice_fusion.2.refs_0_), channel_id=1, source_target_pairs={{0,1},{1,0},{2,3},{3,2},{4,5},{5,4},{6,7},{7,6},{8,9},{9,8},{10,11... | collective-permute-start | bytes 1671176 | tf_op jit(solution)/shard_map/ppermute | solution.py:47
  29.7 4.7 %copy-start.6 = (f32[8192]{0:T(1024)S(1)}, f32[8192]{0:T(1024)}, u32[]{:S(2)}) copy-start(f32[8192]{0:T(1024)} %param.12) | copy-start | bytes 98308
  29.7 4.7 %copy-start.8 = (s32[512]{0:T(512)S(1)}, s32[512]{0:T(512)}, u32[]{:S(2)}) copy-start(s32[512]{0:T(512)} %param.18) | copy-start | bytes 6148
  34.8 2.2 %copy-start = (bf16[1024,8,2,128]{3,1,2,0:T(8,128)(2,1)S(1)}, bf16[1024,8,2,128]{3,1,2,0:T(8,128)(2,1)}, u32[]{:S(2)}) copy-start(bf16[1024,8,2,128]{3,1,2,0:T(8,128)(2,1)} %copy.14) | copy-start | bytes 12582916
  38.0 3.4 %copy-start.1 = (bf16[1024,8,2,128]{3,1,2,0:T(8,128)(2,1)S(1)}, bf16[1024,8,2,128]{3,1,2,0:T(8,128)(2,1)}, u32[]{:S(2)}) copy-start(bf16[1024,8,2,128]{3,1,2,0:T(8,128)(2,1)} %copy.14) | copy-start | bytes 12582916
  38.0 3.4 %copy-start.2 = (f32[128]{0:T(128)S(1)}, f32[128]{0:T(128)}, u32[]{:S(2)}) copy-start(f32[128]{0:T(128)} %param.14) | copy-start | bytes 1540
  41.4 31.4 %copy-start.10 = (s32[8]{0:T(128)S(1)}, s32[8]{0:T(128)}, u32[]{:S(2)}) copy-start(s32[8]{0:T(128)} %constant.152.clone) | copy-start | bytes 100
  41.4 31.4 %copy-start.9 = (s32[16]{0:T(128)S(1)}, s32[16]{0:T(128)}, u32[]{:S(2)}) copy-start(s32[16]{0:T(128)} %param.17) | copy-start | bytes 196
  41.4 32.2 %copy-start.7 = (bf16[16,1024]{1,0:T(8,128)(2,1)S(1)}, bf16[16,1024]{1,0:T(8,128)(2,1)}, u32[]{:S(2)}) copy-start(bf16[16,1024]{1,0:T(8,128)(2,1)} %param.16) | copy-start | bytes 98308
  43.5 7.2 %collective-permute-start.8 = (bf16[256,256]{1,0:T(8,128)(2,1)S(1)}, bf16[256,256]{1,0:T(8,128)(2,1)S(1)}, u32[]{:S(2)}, u32[]{:S(2)}) collective-permute-start(bf16[256,256]{1,0:T(8,128)(2,1)S(1)} %get-tuple-element.22), channel_id=1, source_target_pairs={{0,8},{8,16},{16,24},{24,128},{128,136},{136,144},{144,152},{152,0... | collective-permute-start | bytes 393224 | tf_op jit(solution)/shard_map/ppermute | solution.py:39
  44.6 6.1 %collective-permute-start.9 = (bf16[256,256]{1,0:T(8,128)(2,1)S(1)}, bf16[256,256]{1,0:T(8,128)(2,1)S(1)}, u32[]{:S(2)}, u32[]{:S(2)}) collective-permute-start(bf16[256,256]{1,0:T(8,128)(2,1)S(1)} %get-tuple-element.22), channel_id=1, source_target_pairs={{0,152},{8,0},{16,8},{24,16},{128,24},{136,128},{144,136},{152,144... | collective-permute-start | bytes 393224 | tf_op jit(solution)/shard_map/ppermute | solution.py:39
  50.7 6.3 %collective-permute-start.10 = (bf16[256,256]{1,0:T(8,128)(2,1)S(1)}, bf16[256,256]{1,0:T(8,128)(2,1)S(1)}, u32[]{:S(2)}, u32[]{:S(2)}) collective-permute-start(bf16[256,256]{1,0:T(8,128)(2,1)S(1)} %collective-permute-done.8), channel_id=1, source_target_pairs={{0,8},{8,16},{16,24},{24,128},{128,136},{136,144},{144,152},{152,0... | collective-permute-start | bytes 393224 | tf_op jit(solution)/shard_map/ppermute | solution.py:39
  50.7 6.3 %collective-permute-start.11 = (bf16[256,256]{1,0:T(8,128)(2,1)S(1)}, bf16[256,256]{1,0:T(8,128)(2,1)S(1)}, u32[]{:S(2)}, u32[]{:S(2)}) collective-permute-start(bf16[256,256]{1,0:T(8,128)(2,1)S(1)} %collective-permute-done.9), channel_id=1, source_target_pairs={{0,152},{8,0},{16,8},{24,16},{128,24},{136,128},{144,136},{152,144... | collective-permute-start | bytes 393224 | tf_op jit(solution)/shard_map/ppermute | solution.py:39
  57.0 6.2 %collective-permute-start.12 = (bf16[256,256]{1,0:T(8,128)(2,1)S(1)}, bf16[256,256]{1,0:T(8,128)(2,1)S(1)}, u32[]{:S(2)}, u32[]{:S(2)}) collective-permute-start(bf16[256,256]{1,0:T(8,128)(2,1)S(1)} %collective-permute-done.10), channel_id=1, source_target_pairs={{0,8},{8,16},{16,24},{24,128},{128,136},{136,144},{144,152},{152,0... | collective-permute-start | bytes 393224 | tf_op jit(solution)/shard_map/ppermute | solution.py:39
  57.0 6.2 %collective-permute-start.13 = (bf16[256,256]{1,0:T(8,128)(2,1)S(1)}, bf16[256,256]{1,0:T(8,128)(2,1)S(1)}, u32[]{:S(2)}, u32[]{:S(2)}) collective-permute-start(bf16[256,256]{1,0:T(8,128)(2,1)S(1)} %collective-permute-done.11), channel_id=1, source_target_pairs={{0,152},{8,0},{16,8},{24,16},{128,24},{136,128},{144,136},{152,144... | collective-permute-start | bytes 393224 | tf_op jit(solution)/shard_map/ppermute | solution.py:39
  63.2 5.5 %collective-permute-start.14 = (bf16[128,256]{1,0:T(8,128)(2,1)S(1)}, bf16[128,256]{1,0:T(8,128)(2,1)S(1)}, u32[]{:S(2)}, u32[]{:S(2)}) collective-permute-start(bf16[128,256]{1,0:T(8,128)(2,1)S(1)} %slice.26), channel_id=1, source_target_pairs={{0,8},{8,16},{16,24},{24,128},{128,136},{136,144},{144,152},{152,0... | collective-permute-start | bytes 196616 | tf_op jit(solution)/shard_map/ppermute | solution.py:39
  63.2 5.5 %collective-permute-start.15 = (bf16[128,256]{1,0:T(8,128)(2,1)S(1)}, bf16[128,256]{1,0:T(8,128)(2,1)S(1)}, u32[]{:S(2)}, u32[]{:S(2)}) collective-permute-start(bf16[128,256]{1,0:T(8,128)(2,1)S(1)} %slice.27), channel_id=1, source_target_pairs={{0,152},{8,0},{16,8},{24,16},{128,24},{136,128},{144,136},{152,144... | collective-permute-start | bytes 196616 | tf_op jit(solution)/shard_map/ppermute | solution.py:39
  68.7 29.5 %collective-permute-start.16 = (bf16[2048,256]{1,0:T(8,128)(2,1)S(1)}, bf16[2048,256]{1,0:T(8,128)(2,1)S(1)}, u32[]{:S(2)}, u32[]{:S(2)}) collective-permute-start(bf16[2048,256]{1,0:T(8,128)(2,1)S(1)} %constant_dynamic-update-slice_fusion.4.refs_0_), channel_id=1, source_target_pairs={{0,32},{8,40},{16,48},{24,56},{128,160},{136,168},{144,176},{152,1... | collective-permute-start | bytes 3145736 | tf_op jit(solution)/shard_map/ppermute | solution.py:39
  69.0 31.3 %collective-permute-start.18 = (bf16[2048,256]{1,0:T(8,128)(2,1)S(1)}, bf16[2048,256]{1,0:T(8,128)(2,1)S(1)}, u32[]{:S(2)}, u32[]{:S(2)}) collective-permute-start(bf16[2048,256]{1,0:T(8,128)(2,1)S(1)} %constant_dynamic-update-slice_fusion.4.refs_0_), channel_id=1, source_target_pairs={{0,96},{8,104},{16,112},{24,120},{128,224},{136,232},{144,240},{15... | collective-permute-start | bytes 3145736 | tf_op jit(solution)/shard_map/ppermute | solution.py:39
  70.8 8.3 %collective-permute-start.20 = (bf16[16,256]{1,0:T(8,128)(2,1)S(1)}, bf16[16,256]{1,0:T(8,128)(2,1)S(1)}, u32[]{:S(2)}, u32[]{:S(2)}) collective-permute-start(bf16[16,256]{1,0:T(8,128)(2,1)S(1)} %get-tuple-element.23), channel_id=1, source_target_pairs={{0,8},{8,16},{16,24},{24,32},{32,40},{40,48},{48,56},{56,64},{64,7... | collective-permute-start | bytes 24584 | tf_op jit(solution)/shard_map/ppermute | solution.py:377
  79.3 1.1 copy-start.3
  96.8 1.4 copy-start.5
  98.2 33.9 %collective-permute-start.17 = (bf16[1024,256]{1,0:T(8,128)(2,1)S(1)}, bf16[1024,256]{1,0:T(8,128)(2,1)S(1)}, u32[]{:S(2)}, u32[]{:S(2)}) collective-permute-start(bf16[1024,256]{1,0:T(8,128)(2,1)S(1)} %slice.28), channel_id=1, source_target_pairs={{0,32},{8,40},{16,48},{24,56},{128,160},{136,168},{144,176},{152,1... | collective-permute-start | bytes 1572872 | tf_op jit(solution)/shard_map/ppermute | solution.py:39
  100.4 31.7 %collective-permute-start.19 = (bf16[1024,256]{1,0:T(8,128)(2,1)S(1)}, bf16[1024,256]{1,0:T(8,128)(2,1)S(1)}, u32[]{:S(2)}, u32[]{:S(2)}) collective-permute-start(bf16[1024,256]{1,0:T(8,128)(2,1)S(1)} %slice.29), channel_id=1, source_target_pairs={{0,96},{8,104},{16,112},{24,120},{128,224},{136,232},{144,240},{15... | collective-permute-start | bytes 1572872 | tf_op jit(solution)/shard_map/ppermute | solution.py:39
  132.1 1.6 %copy-start.4 = (f32[2048,256]{1,0:T(8,128)S(1)}, f32[2048,256]{1,0:T(8,128)}, u32[]{:S(2)}) copy-start(f32[2048,256]{1,0:T(8,128)} %get-tuple-element.29.refs_6_) | copy-start | bytes 6291460
